TPU v7x, 32 devices: a whole 2x2x4 slice. The times are simulated.
32 devices in a mesh: replica: 4 (over y, x), shard: 8 (over z, core).
Axes of the slice: x: 2, y: 2, z: 4, core: 2. Of those that a mesh axis runs over, the one named last changes fastest.
Arguments:
- tokens: bfloat16 [4096, 8192], P(('replica', 'shard')), may hold values from -6 to 6
- cotangent: bfloat16 [4096, 512], P(('replica', 'shard')), may hold values from -6 to 6
- biased: float32 [4, 8192, 512], P('replica', 'shard'), may hold values from -0.0625 to 0.0625
- momentum: float32 [4, 8192, 512], P('replica', 'shard'), may hold values from -0.12 to 0.12
- weight: float32 [4], P('replica'), may hold values from 0.25 to 4
- round_index: int32 [1], replicated, may hold values from 0 to 999999
Outputs:
- projected: bfloat16 [4096, 512], P(('replica', 'shard'))
- mixed: float32 [4, 8192, 512], P('replica', 'shard')
- weight_out: float32 [4], P('replica')
- velocity: float32 [4, 8192, 512], P('replica', 'shard')
- debiased: float32 [4, 8192, 512], P('replica', 'shard')
Inputs may be any that keep to these rules, and one draw needn't show every extreme that they name: `round_index`: any round number.
All inputs are finite; a program needn't handle non-finite values.
Results may differ from a plain program's by a relative error of at most 0.005.
Values may be sent and summed in bfloat16 or wider, within the bound.
A program may use at most 64 MiB of HBM per device.

v0:
```python
from functools import partial

import jax
import jax.numpy as jnp
from jax import lax
from jax.sharding import PartitionSpec as P

MOMENT = 0.9
LEARN = 0.5


def shifted(block, axis, distance):
    devices = range(lax.axis_size(axis))
    route = [((i - distance) % len(devices), i) for i in devices]
    return lax.ppermute(block, axis, route)


def send_push(dist, payload):
    return shifted(payload, "replica", dist)


def shards(tokens, cotangent, biased, momentum, weight, round_index):
    hops = lax.axis_size("replica").bit_length() - 1
    power = round_index[0] % hops
    numer = biased[0]
    scale = weight[0]
    rep_tokens = tokens.shape[0] * lax.axis_size("shard")
    current = (numer / scale).astype(jnp.bfloat16)
    full_rows = lax.all_gather(current, "shard", axis=0, tiled=True)
    output = jnp.dot(tokens, full_rows, preferred_element_type=jnp.float32)
    feature_cols = lax.all_to_all(tokens, "shard", split_axis=1, concat_axis=0, tiled=True)
    contract = (((0,), (0,)), ((), ()))
    all_cots = lax.all_gather(cotangent, "shard", axis=0, tiled=True)
    gradient = lax.dot_general(feature_cols, all_cots, contract, preferred_element_type=jnp.float32)
    gradient = gradient / rep_tokens
    velocity = MOMENT * momentum[0] + gradient
    nesterov = gradient + MOMENT * velocity
    stepped = numer - LEARN * nesterov
    branches = [partial(send_push, 1 << level) for level in range(hops)]
    stepped_from, weight_from = lax.switch(power, branches, (stepped, weight))
    mixed = 0.5 * (stepped + stepped_from)
    weight_out = 0.5 * (weight + weight_from)
    debiased = mixed / weight_out[0]
    return (output.astype(jnp.bfloat16), mixed[None], weight_out, velocity[None], debiased[None])


def solution(mesh):
    placed = (
        P(("replica", "shard"), None),
        P(("replica", "shard"), None),
        P("replica", "shard", None),
        P("replica", "shard", None),
        P("replica"),
        P(),
    )
    return jax.shard_map(
        shards,
        mesh=mesh,
        in_specs=placed,
        out_specs=(
            P(("replica", "shard"), None),
            P("replica", "shard", None),
            P("replica"),
            P("replica", "shard", None),
            P("replica", "shard", None),
        ),
        check_vma=False,
    )
```

profile of v0, /device:TPU:0, one launch (start us, length us, event | category | flops | bytes accessed | tf_op | source)
XLA Modules:
  0.0 180.4 jit_solution(6366515881409999648)
XLA Ops:
  7.2 4.1 %copy.13 = bf16[128,8192]{0,1:T(8,128)(2,1)} copy(bf16[128,8192]{1,0:T(8,128)(2,1)} %param.8) | data formatting | bytes 4194304 | tf_op args[0]
  11.2 6.3 %all-to-all-start = ((bf16[128,8,1024]{0,2,1:T(8,128)(2,1)}), bf16[128,8,1024]{0,2,1:T(8,128)(2,1)S(1)}, u32[]{:S(2)}, u32[]{:S(2)}) async-start(bf16[128,8,1024]{0,2,1:T(8,128)(2,1)} %bitcast.34), calls=%async_computation | async-start | bytes 4194304 | tf_op jit(solution)/shard_map/all_to_all | solution.py:31
  17.6 0.0 all-gather.5.cloned.1.call-start
  17.6 0.7 all-gather.5.cloned.1.call-update
  18.3 0.0 all-gather.3.cloned.1.call-start
  19.0 56.1 %all-to-all-done = bf16[128,8,1024]{0,2,1:T(8,128)(2,1)S(1)} async-done(((bf16[128,8,1024]{0,2,1:T(8,128)(2,1)}), bf16[128,8,1024]{0,2,1:T(8,128)(2,1)S(1)}, u32[]{:S(2)}, u32[]{:S(2)}) %all-to-all-start) | async-done | bytes 2097184 | tf_op jit(solution)/shard_map/all_to_all | solution.py:31
  75.1 2.6 %copy.14 = bf16[8,128,1024]{2,1,0:T(8,128)(2,1)} copy(bf16[8,128,1024]{1,2,0:T(8,128)(2,1)S(1)} %bitcast.33) | data formatting | bytes 4194304 | tf_op jit(solution)/shard_map/all_to_all | solution.py:31
  77.6 0.0 all-gather.5.cloned.1.call-done
  77.6 7.2 %fusion.1 = (f32[1,1024,512]{2,1,0:T(8,128)}, f32[1024,512]{1,0:T(8,128)}, bf16[1024,512]{1,0:T(8,128)(2,1)}) fusion(f32[1,1024,512]{2,1,0:T(8,128)} %param.11, f32[1,1024,512]{2,1,0:T(8,128)} %param.10, f32[]{:T(128)} %bitcast.29, bf16[1024,1024]{1,0:T(8,128)(2,1)} %bitcast.35, bf16[1024,512]{1,0:T(8,128)(2,1)} %all-gather.5.cloned.1.call-done), kind=kOutput, calls=%fused_computation.6 | convolution fusion | flops 1078460416 | bytes 12582916 | tf_op jit(solution)/shard_map/dot_general | solution.py:34
  84.8 0.0 all-gather.3.cloned.1.call-update
  85.5 47.6 %conditional.1 = (f32[1024,512]{1,0:T(8,128)}, f32[1]{0:T(128)}) conditional(s32[]{:T(128)} %clamp.3, (f32[1024,512]{1,0:T(8,128)}, f32[1]{0:T(128)}) %tuple.16, (f32[1024,512]{1,0:T(8,128)}, f32[1]{0:T(128)}) %tuple.16), branch_computations={%region_0.1_spmd, %region_1.2_spmd} | conditional | bytes 8388720 | solution.py:40
  85.5 1.6 collective-permute-start.2
  87.1 0.5 collective-permute-start.3
  87.6 45.5 %collective-permute-done.3 = f32[1]{0:T(128)} collective-permute-done((f32[1]{0:T(128)}, f32[1]{0:T(128)}, u32[]{:S(2)}, u32[]{:S(2)}) %collective-permute-start.3) | collective-permute-done | bytes 36 | tf_op jit(solution)/shard_map/cond/branch_1_fun/ppermute | solution.py:15
  133.1 0.0 collective-permute-done.2
  133.8 0.0 copy-start
  133.8 5.0 %divide_bitcast_fusion = (f32[1,1024,512]{2,1,0:T(8,128)}, f32[1,1024,512]{2,1,0:T(8,128)}) fusion(f32[]{:T(128)} %bitcast.10, f32[1024,512]{1,0:T(8,128)} %get-tuple-element.39, f32[1024,512]{1,0:T(8,128)} %get-tuple-element.19), kind=kLoop, calls=%fused_computation.4 | loop fusion | flops 1572864 | bytes 8388612 | tf_op jit(solution)/shard_map/broadcast_in_dim | solution.py:44
  138.8 27.2 %all-gather.3.cloned.1.call-done = bf16[8192,512]{1,0:T(8,128)(2,1)} async-done(((bf16[1024,512]{1,0:T(8,128)(2,1)}), bf16[8192,512]{1,0:T(8,128)(2,1)}) %all-gather.3.cloned.1.call-update) | async-done | bytes 8388624 | tf_op jit(solution)/shard_map/all_gather | solution.py:29
  165.9 0.0 copy-done
  165.9 5.8 %fusion.2 = bf16[128,512]{0,1:T(8,128)(2,1)S(1)} fusion(bf16[8192,512]{1,0:T(8,128)(2,1)} %all-gather.3.cloned.1.call-done, bf16[128,8192]{1,0:T(8,128)(2,1)S(1)} %copy-done), kind=kOutput, calls=%fused_computation.8 | convolution fusion | flops 1073807360 | bytes 10616832 | tf_op jit(solution)/shard_map/dot_general | solution.py:30
  171.7 0.8 copy.15
Async XLA Ops:
  11.2 63.8 %all-to-all-start = ((bf16[128,8,1024]{0,2,1:T(8,128)(2,1)}), bf16[128,8,1024]{0,2,1:T(8,128)(2,1)S(1)}, u32[]{:S(2)}, u32[]{:S(2)}) async-start(bf16[128,8,1024]{0,2,1:T(8,128)(2,1)} %bitcast.34), calls=%async_computation | async-start | bytes 4194304 | tf_op jit(solution)/shard_map/all_to_all | solution.py:31
  17.6 60.1 %all-gather.5.cloned.1.call-start = ((), (), s32[]{:S(2)}) async-start(), calls=%async_computation.2 | async-start | bytes 1179648 | tf_op jit(solution)/shard_map/all_gather | solution.py:33
  18.3 147.6 %all-gather.3.cloned.1.call-start = ((), (), s32[]{:S(2)}) async-start(), calls=%async_computation.1 | async-start | bytes 9437184 | tf_op jit(solution)/shard_map/all_gather | solution.py:29
  85.5 47.6 %collective-permute-start.2 = (f32[1024,512]{1,0:T(8,128)}, f32[1024,512]{1,0:T(8,128)}, u32[]{:S(2)}, u32[]{:S(2)}) collective-permute-start(f32[1024,512]{1,0:T(8,128)} %get-tuple-element.10), channel_id=1, source_target_pairs={{16,0},{24,8},{0,16},{8,24},{17,1},{25,9},{1,17},{9,25},{18,2},{26... | collective-permute-start | bytes 6291464 | tf_op jit(solution)/shard_map/cond/branch_1_fun/ppermute | solution.py:15
  87.1 46.0 %collective-permute-start.3 = (f32[1]{0:T(128)}, f32[1]{0:T(128)}, u32[]{:S(2)}, u32[]{:S(2)}) collective-permute-start(f32[1]{0:T(128)} %get-tuple-element.11), channel_id=1, source_target_pairs={{16,0},{24,8},{0,16},{8,24},{17,1},{25,9},{1,17},{9,25},{18,2},{26... | collective-permute-start | bytes 20 | tf_op jit(solution)/shard_map/cond/branch_1_fun/ppermute | solution.py:15
  133.8 32.2 %copy-start = (bf16[128,8192]{1,0:T(8,128)(2,1)S(1)}, bf16[128,8192]{1,0:T(8,128)(2,1)}, u32[]{:S(2)}) copy-start(bf16[128,8192]{1,0:T(8,128)(2,1)} %param.8) | copy-start | bytes 6291460
Sparse Core Ops, SparseCore 0:
  20.0 31.2 all-gather.4
  84.9 80.9 all-gather.2
where the time goes:
time: 181 us; the launch traced here: 180 us
  waiting for transfers between devices  129 us (71%)
  between operations  17.1 us (9%)
  matrix products  12.9 us (7%)
  starting transfers between devices  8.49 us (5%)
  local copies, waits for them, and re-layouts  7.43 us (4%)
  other arithmetic  5 us (3%)
    all_to_all x1, waiting for transfers between devices, shards(): lax.all_to_all(tokens, 'shard', split_axis=1, concat_axis=0, tiled=True)  56.1 us
    ppermute x2, waiting for transfers between devices, shifted(): return lax.ppermute(block, axis, route)  45.5 us
    all_gather x1, waiting for transfers between devices, shards(): full_rows = lax.all_gather(current, 'shard', axis=0, tiled=True)  27.2 us
    dot_general x1, matrix products, shards(): lax.dot_general(feature_cols, all_cots, contract, preferred_element_type=...  7.16 us
    all_to_all x1, starting transfers between devices, shards(): lax.all_to_all(tokens, 'shard', split_axis=1, concat_axis=0, tiled=True)  6.33 us
    dot_general x1, matrix products, shards(): output = jnp.dot(tokens, full_rows, preferred_element_type=jnp.float32)  5.76 us
    broadcast_in_dim x1, other arithmetic, shards(): debiased[None]  5 us
    unnamed x4, local copies, waits for them, and re-layouts  4.85 us
  transfers between devices with their start and end apart: 5, of which 3 were waited for; matrix products, arithmetic and copies ran while one was open for 4% of the time, Pallas kernels for 0%

commit v1 on v0

v1 whole, which is shorter than its diff:
```python
from functools import partial

import jax
import jax.numpy as jnp
from jax import lax
from jax.experimental import pallas as pl
from jax.experimental.pallas import tpu as pltpu
from jax.sharding import PartitionSpec as P

MOMENT = 0.9
LEARN = 0.5
MESH = pl.DeviceIdType.MESH
CORES = 2
BF16 = jnp.bfloat16
F32 = jnp.float32


def flipped(z, x, chips):
    total, bit = 0, 1
    while bit < chips:
        total = total + bit * ((z // bit + x // bit) % 2)
        bit *= 2
    return total


def partners(chips):
    order, bit = [], chips // 2
    while bit >= 1:
        order += list(range(bit, 2 * bit))
        bit //= 2
    return order


def push_kernel(dist, chips, nk, tok, cot, biased, momentum, weight,
                p_out, g_out, s_out, w_out,
                t_v, c_v, b_v, m_v, cur, acc, p_send, p_recv, gp_send, gp_recv, g_v, s_send, w_send,
                load_sem, own_sem, c_ssem, c_rsem, t_ssem, t_rsem, cur_ssem, cur_rsem,
                gp_ssem, gp_rsem, s_ssem, s_rsem, p_ssem, p_rsem, w_ssem, w_rsem, store_sem):
    rows, kv = b_v.shape
    own_tok = tok.shape[0]
    width = rows // nk
    rep_tok = own_tok * chips * CORES
    replicas = lax.axis_size("replica")
    rep = lax.axis_index("replica")
    shard = lax.axis_index("shard")
    z = shard // CORES
    c = shard % CORES
    other = 1 - c
    mate = z * CORES + other
    ahead = (rep + dist) % replicas
    behind = (rep + replicas - dist) % replicas
    order = partners(chips)
    peers = [flipped(z, x, chips) for x in order]

    loads = [
        pltpu.make_async_copy(biased, b_v, load_sem.at[0]),
        pltpu.make_async_copy(momentum, m_v, load_sem.at[1]),
        pltpu.make_async_copy(cot, c_v.at[z], load_sem.at[2]),
    ]
    for load in loads:
        load.start()

    def columns(chip, half, k):
        return pl.ds(pl.multiple_of((chip * CORES + half) * rows + k * width, width), width)

    def own_copy(k, half):
        return pltpu.make_async_copy(tok.at[:, columns(z, half, k)], t_v.at[k, half, z], own_sem.at[k, half])

    def tok_copy(k, half, j):
        return pltpu.make_async_remote_copy(
            src_ref=tok.at[:, columns(peers[j], half, k)], dst_ref=t_v.at[k, half, z],
            send_sem=t_ssem.at[k, half, j], recv_sem=t_rsem.at[k, half, j],
            device_id={"shard": peers[j] * CORES + c}, device_id_type=MESH)

    def cot_copy(j):
        return pltpu.make_async_remote_copy(
            src_ref=cot, dst_ref=c_v.at[z], send_sem=c_ssem.at[j], recv_sem=c_rsem.at[j],
            device_id={"shard": peers[j] * CORES + c}, device_id_type=MESH)

    def p_copy(j):
        return pltpu.make_async_remote_copy(
            src_ref=p_send.at[j], dst_ref=p_recv.at[j], send_sem=p_ssem.at[j], recv_sem=p_rsem.at[j],
            device_id={"shard": peers[j] * CORES + c}, device_id_type=MESH)

    def gp_copy(k):
        return pltpu.make_async_remote_copy(
            src_ref=gp_send.at[k], dst_ref=gp_recv.at[k], send_sem=gp_ssem.at[k], recv_sem=gp_rsem.at[k],
            device_id={"shard": mate}, device_id_type=MESH)

    def s_copy(k):
        return pltpu.make_async_remote_copy(
            src_ref=s_send.at[k], dst_ref=s_out.at[pl.ds(pl.multiple_of(k * width, width), width), :],
            send_sem=s_ssem.at[k], recv_sem=s_rsem.at[k],
            device_id={"replica": ahead}, device_id_type=MESH)

    def g_store(k):
        return pltpu.make_async_copy(
            g_v.at[k], g_out.at[pl.ds(pl.multiple_of(k * width, width), width), :], store_sem.at[k])

    for k in range(nk):
        for half in range(CORES):
            own_copy(k, half).start()

    barrier = pltpu.get_barrier_semaphore()
    for peer in peers:
        pl.semaphore_signal(barrier, inc=1, device_id={"shard": peer * CORES + c}, device_id_type=MESH)
    pl.semaphore_signal(barrier, inc=1, device_id={"shard": mate}, device_id_type=MESH)
    pl.semaphore_signal(barrier, inc=1, device_id={"replica": behind}, device_id_type=MESH)
    pl.semaphore_wait(barrier, len(peers) + 2)

    for j in range(len(peers)):
        cot_copy(j).start()
    for k in range(nk):
        for j in range(len(peers)):
            for half in range(CORES):
                tok_copy(k, half, j).start()

    w_send[...] = jnp.full(w_send.shape, weight[0], F32)
    w_copy = pltpu.make_async_remote_copy(
        src_ref=w_send, dst_ref=w_out, send_sem=w_ssem, recv_sem=w_rsem,
        device_id={"replica": ahead}, device_id_type=MESH)
    w_copy.start()

    loads[0].wait()
    mine = cur.at[c]
    mine[...] = (b_v[...] / weight[0]).astype(BF16)
    cur_copy = pltpu.make_async_remote_copy(
        src_ref=mine, dst_ref=mine, send_sem=cur_ssem, recv_sem=cur_rsem,
        device_id={"shard": mate}, device_id_type=MESH)
    cur_copy.start()
    acc[...] = jnp.zeros(acc.shape, F32)
    loads[1].wait()
    loads[2].wait()
    for j in range(len(peers)):
        cot_copy(j).wait_recv()
    cur_copy.wait_recv()

    contract = (((0,), (0,)), ((), ()))

    def arrived(k):
        for half in range(CORES):
            own_copy(k, half).wait()
        for j in range(len(peers)):
            for half in range(CORES):
                tok_copy(k, half, j).wait_recv()

    def partial_gradient(k, half):
        t = t_v[k, half].reshape(chips * own_tok, width)
        cots = c_v[...].reshape(chips * own_tok, kv)
        return lax.dot_general(t, cots, contract, preferred_element_type=F32)

    def product(k, t):
        here = pl.ds(pl.multiple_of(k * width, width), width)
        return (jnp.dot(t[0], cur[0, here, :], preferred_element_type=F32)
                + jnp.dot(t[1], cur[1, here, :], preferred_element_type=F32))

    def send_gradient(k):
        gp_send[k] = partial_gradient(k, other).astype(BF16)
        gp_copy(k).start()
        g_v[k] = partial_gradient(k, c)

    def finish_gradient(k):
        here = pl.ds(pl.multiple_of(k * width, width), width)
        gp_copy(k).wait_recv()
        gradient = (g_v[k] + gp_recv[k].astype(F32)) / rep_tok
        g_v[k] = gradient
        velocity = MOMENT * m_v[here, :] + gradient
        s_send[k] = (b_v[here, :] - LEARN * (gradient + MOMENT * velocity)).astype(BF16)
        s_copy(k).start()
        g_store(k).start()

    if nk > 1:
        @pl.loop(0, nk - 1)
        def _(k):
            arrived(k)
            send_gradient(k)
            for s in range(chips):
                acc[s] += product(k, (t_v[k, 0, s], t_v[k, 1, s]))
            finish_gradient(k)

    last = nk - 1
    arrived(last)
    send_gradient(last)
    for j in range(len(peers)):
        s = peers[j]
        p_send[j] = (acc[s] + product(last, (t_v[last, 0, s], t_v[last, 1, s]))).astype(BF16)
        p_copy(j).start()
    finish_gradient(last)
    total = acc[z] + product(last, (t_v[last, 0, z], t_v[last, 1, z]))
    for j in range(len(peers)):
        p_copy(j).wait_recv()
        total = total + p_recv[j].astype(F32)
    p_send[len(peers)] = total.astype(BF16)
    p_store = pltpu.make_async_copy(p_send.at[len(peers)], p_out, store_sem.at[nk])
    p_store.start()

    for j in range(len(peers)):
        cot_copy(j).wait_send()
        p_copy(j).wait_send()
        for k in range(nk):
            for half in range(CORES):
                tok_copy(k, half, j).wait_send()
    cur_copy.wait_send()
    for k in range(nk):
        gp_copy(k).wait_send()
        s_copy(k).wait()
        g_store(k).wait()
    w_copy.wait()
    p_store.wait()


def push_call(level, chips, tokens, cotangent, numer, moment, weight):
    own_tok, features = tokens.shape
    rows, kv = numer.shape
    nk = max(1, rows // 256)
    width = rows // nk
    n = chips - 1
    any_spec = pl.BlockSpec(memory_space=pl.ANY)
    dma = pltpu.SemaphoreType.DMA
    return pl.pallas_call(
        partial(push_kernel, 1 << level, chips, nk),
        out_shape=(
            jax.ShapeDtypeStruct((own_tok, kv), BF16),
            jax.ShapeDtypeStruct((rows, kv), F32),
            jax.ShapeDtypeStruct((rows, kv), BF16),
            jax.ShapeDtypeStruct((8, 128), F32),
        ),
        in_specs=[any_spec] * 4 + [pl.BlockSpec(memory_space=pltpu.SMEM)],
        out_specs=[any_spec] * 4,
        scratch_shapes=[
            pltpu.VMEM((nk, CORES, chips, own_tok, width), BF16),
            pltpu.VMEM((chips, own_tok, kv), BF16),
            pltpu.VMEM((rows, kv), F32),
            pltpu.VMEM((rows, kv), F32),
            pltpu.VMEM((CORES, rows, kv), BF16),
            pltpu.VMEM((chips, own_tok, kv), F32),
            pltpu.VMEM((chips, own_tok, kv), BF16),
            pltpu.VMEM((n, own_tok, kv), BF16),
            pltpu.VMEM((nk, width, kv), BF16),
            pltpu.VMEM((nk, width, kv), BF16),
            pltpu.VMEM((nk, width, kv), F32),
            pltpu.VMEM((nk, width, kv), BF16),
            pltpu.VMEM((8, 128), F32),
            dma((3,)), dma((nk, CORES)), dma((n,)), dma((n,)), dma((nk, CORES, n)), dma((nk, CORES, n)),
            dma(()), dma(()), dma((nk,)), dma((nk,)), dma((nk,)), dma((nk,)), dma((n,)), dma((n,)),
            dma(()), dma(()), dma((nk + 1,)),
        ],
        compiler_params=pltpu.CompilerParams(
            collective_id=level, has_side_effects=True, vmem_limit_bytes=48 * 1024 * 1024),
        cost_estimate=pl.CostEstimate(
            flops=4 * own_tok * features * kv, bytes_accessed=12 * rows * kv, transcendentals=0),
        name=f"push_round_{level}",
    )(tokens, cotangent, numer, moment, weight)


def shards(tokens, cotangent, biased, momentum, weight, round_index):
    hops = lax.axis_size("replica").bit_length() - 1
    chips = lax.axis_size("shard") // CORES
    power = round_index[0] % hops
    numer = biased[0]
    moment = momentum[0]
    branches = [partial(push_call, level, chips) for level in range(hops)]
    output, gradient, stepped_from, weight_from = lax.switch(
        power, branches, tokens, cotangent, numer, moment, weight)
    velocity = MOMENT * moment + gradient
    stepped = numer - LEARN * (gradient + MOMENT * velocity)
    mixed = 0.5 * (stepped + stepped_from.astype(F32))
    weight_out = 0.5 * (weight + weight_from[0, :1])
    debiased = mixed / weight_out[0]
    return (output, mixed[None], weight_out, velocity[None], debiased[None])


def solution(mesh):
    placed = (
        P(("replica", "shard"), None),
        P(("replica", "shard"), None),
        P("replica", "shard", None),
        P("replica", "shard", None),
        P("replica"),
        P(),
    )
    return jax.shard_map(
        shards,
        mesh=mesh,
        in_specs=placed,
        out_specs=(
            P(("replica", "shard"), None),
            P("replica", "shard", None),
            P("replica"),
            P("replica", "shard", None),
            P("replica", "shard", None),
        ),
        check_vma=False,
    )
```

time: 181 us -> 87.5 us (0.48)
  the two profiles are of different devices: /device:TPU:0 before, /device:TPU:17 now
where the time goes in v1:
time: 87.5 us; the launch traced here: 87.8 us
  Pallas kernels  76.8 us (88%)
  other arithmetic  6.08 us (7%)
  between operations  3.73 us (4%)
  local copies, waits for them, and re-layouts  1.17 us (1%)
    pallas_call x1, Pallas kernels, push_call(): pl.pallas_call(partial(push_kernel, 1 << level, chips, nk), out_shape=(ja...  76.8 us
    broadcast_in_dim x1, other arithmetic, shards(): return (output, mixed[None], weight_out, velocity[None], debiased[None])  6.08 us

profile of v1, /device:TPU:17, one launch (start us, length us, event | category | flops | bytes accessed | tf_op | source)
XLA Modules:
  0.0 87.8 jit_solution(9788021225300887415)
XLA Ops:
  1.9 76.8 %conditional.1 = ((bf16[128,512]{1,0:T(8,128)(2,1)S(1)}, f32[1024,512]{1,0:T(8,128)S(1)}, bf16[1024,512]{1,0:T(8,128)(2,1)S(1)}, f32[8,128]{1,0:T(8,128)S(1)})) conditional(s32[]{:T(128)} %clamp.3, (bf16[128,8192]{1,0:T(8,128)(2,1)}, bf16[128,512]{1,0:T(8,128)(2,1)}, f32[1024,512]{1,0:T(8,128)}, f32[1024,512]{1,0:T(8,128)}, f32[1]{0:T(128)}) %tuple.40, ...), branch_computations={%region_0.1_spmd, %region_1.2_spmd} | conditional | flops 2147483648 | bytes 6291464 | solution.py:263
  2.0 76.8 %push_round_0.1 = (bf16[128,512]{1,0:T(8,128)(2,1)S(1)}, f32[1024,512]{1,0:T(8,128)S(1)}, bf16[1024,512]{1,0:T(8,128)(2,1)S(1)}, f32[8,128]{1,0:T(8,128)S(1)}) custom-call(bf16[128,8192]{1,0:T(8,128)(2,1)} %get-tuple-element.72.tok, bf16[128,512]{1,0:T(8,128)(2,1)} %get-tuple-element.74.cot, f32[1024,512]{1,0:T(8,128)} %get-tuple-element.37.biased, ...), custom_call_target="tpu_custom_call" | custom-call | flops 2147483648 | bytes 6291456 | tf_op jit(solution)/shard_map/cond/branch_0_fun/push_round_0/pallas_call | solution.py:220
  78.7 0.5 slice.9
  79.9 6.1 %divide_bitcast_fusion = (f32[1,1024,512]{2,1,0:T(8,128)}, f32[1024,512]{1,0:T(8,128)}, f32[1,1024,512]{2,1,0:T(8,128)}) fusion(f32[]{:T(128)} %bitcast.6, bf16[1024,512]{1,0:T(8,128)(2,1)S(1)} %get-tuple-element.78, f32[1024,512]{1,0:T(8,128)S(1)} %get-tuple-element.79, f32[1,1024,512]{2,1,0:T(8,128)} %param.11, f32[1,1024,512]{2,1,0:T(8,128)} %param.10), kind=kLoop, calls=%fused_computation.2 | loop fusion | flops 5242880 | bytes 13631492 | tf_op jit(solution)/shard_map/broadcast_in_dim | solution.py:270
  86.0 0.7 copy.26

commit v2 on v1

--- a/solution.py
+++ b/solution.py
@@ -32,8 +32,9 @@
 
 
 def push_kernel(dist, chips, nk, tok, cot, biased, momentum, weight,
-                p_out, g_out, s_out, w_out,
-                t_v, c_v, b_v, m_v, cur, acc, p_send, p_recv, gp_send, gp_recv, g_v, s_send, w_send,
+                p_out, mix_out, w_out, vel_out, deb_out,
+                t_v, c_v, b_v, m_v, cur, acc, p_send, p_recv, gp_send, gp_recv, g_v, s_send, s_recv, deb_v,
+                w_send, w_recv,
                 load_sem, own_sem, c_ssem, c_rsem, t_ssem, t_rsem, cur_ssem, cur_rsem,
                 gp_ssem, gp_rsem, s_ssem, s_rsem, p_ssem, p_rsem, w_ssem, w_rsem, store_sem):
     rows, kv = b_v.shape
@@ -72,10 +73,12 @@
             send_sem=t_ssem.at[k, half, j], recv_sem=t_rsem.at[k, half, j],
             device_id={"shard": peers[j] * CORES + c}, device_id_type=MESH)
 
-    def cot_copy(j):
-        return pltpu.make_async_remote_copy(
-            src_ref=cot, dst_ref=c_v.at[z], send_sem=c_ssem.at[j], recv_sem=c_rsem.at[j],
-            device_id={"shard": peers[j] * CORES + c}, device_id_type=MESH)
+    def cot_copy(x):
+        low = x & -x
+        held = z if x == low else flipped(z, x - low, chips)
+        return pltpu.make_async_remote_copy(
+            src_ref=c_v.at[held], dst_ref=c_v.at[held], send_sem=c_ssem.at[x], recv_sem=c_rsem.at[x],
+            device_id={"shard": flipped(z, low, chips) * CORES + c}, device_id_type=MESH)
 
     def p_copy(j):
         return pltpu.make_async_remote_copy(
@@ -89,13 +92,14 @@
 
     def s_copy(k):
         return pltpu.make_async_remote_copy(
-            src_ref=s_send.at[k], dst_ref=s_out.at[pl.ds(pl.multiple_of(k * width, width), width), :],
+            src_ref=s_send.at[k], dst_ref=s_recv.at[k],
             send_sem=s_ssem.at[k], recv_sem=s_rsem.at[k],
             device_id={"replica": ahead}, device_id_type=MESH)
 
-    def g_store(k):
-        return pltpu.make_async_copy(
-            g_v.at[k], g_out.at[pl.ds(pl.multiple_of(k * width, width), width), :], store_sem.at[k])
+    def store(k, i):
+        here = pl.ds(pl.multiple_of(k * width, width), width)
+        made, out = ((m_v, vel_out), (b_v, mix_out), (deb_v, deb_out))[i]
+        return pltpu.make_async_copy(made.at[here, :], out.at[here, :], store_sem.at[k, i])
 
     for k in range(nk):
         for half in range(CORES):
@@ -108,8 +112,8 @@
     pl.semaphore_signal(barrier, inc=1, device_id={"replica": behind}, device_id_type=MESH)
     pl.semaphore_wait(barrier, len(peers) + 2)
 
-    for j in range(len(peers)):
-        cot_copy(j).start()
+    loads[2].wait()
+    cot_copy(chips // 2).start()
     for k in range(nk):
         for j in range(len(peers)):
             for half in range(CORES):
@@ -117,7 +121,7 @@
 
     w_send[...] = jnp.full(w_send.shape, weight[0], F32)
     w_copy = pltpu.make_async_remote_copy(
-        src_ref=w_send, dst_ref=w_out, send_sem=w_ssem, recv_sem=w_rsem,
+        src_ref=w_send, dst_ref=w_recv, send_sem=w_ssem, recv_sem=w_rsem,
         device_id={"replica": ahead}, device_id_type=MESH)
     w_copy.start()
 
@@ -130,10 +134,20 @@
     cur_copy.start()
     acc[...] = jnp.zeros(acc.shape, F32)
     loads[1].wait()
-    loads[2].wait()
-    for j in range(len(peers)):
-        cot_copy(j).wait_recv()
+    bit = chips // 4
+    while bit >= 1:
+        for x in range(2 * bit, chips, 4 * bit):
+            cot_copy(x).wait_recv()
+        for x in range(bit, chips, 2 * bit):
+            cot_copy(x).start()
+        bit //= 2
+    for x in range(1, chips, 2):
+        cot_copy(x).wait_recv()
     cur_copy.wait_recv()
+    w_copy.wait()
+    w_send[...] = 0.5 * (w_send[...] + w_recv[...])
+    w_store = pltpu.make_async_copy(w_send, w_out, w_ssem)
+    w_store.start()
 
     contract = (((0,), (0,)), ((), ()))
 
@@ -163,11 +177,22 @@
         here = pl.ds(pl.multiple_of(k * width, width), width)
         gp_copy(k).wait_recv()
         gradient = (g_v[k] + gp_recv[k].astype(F32)) / rep_tok
-        g_v[k] = gradient
         velocity = MOMENT * m_v[here, :] + gradient
-        s_send[k] = (b_v[here, :] - LEARN * (gradient + MOMENT * velocity)).astype(BF16)
+        m_v[here, :] = velocity
+        stepped = b_v[here, :] - LEARN * (gradient + MOMENT * velocity)
+        b_v[here, :] = stepped
+        s_send[k] = stepped.astype(BF16)
         s_copy(k).start()
-        g_store(k).start()
+        store(k, 0).start()
+
+    def mix(k):
+        here = pl.ds(pl.multiple_of(k * width, width), width)
+        s_copy(k).wait_recv()
+        mixed = 0.5 * (b_v[here, :] + s_recv[k].astype(F32))
+        b_v[here, :] = mixed
+        deb_v[here, :] = mixed / w_send[0:1, 0:1]
+        store(k, 1).start()
+        store(k, 2).start()
 
     if nk > 1:
         @pl.loop(0, nk - 1)
@@ -178,6 +203,10 @@
                 acc[s] += product(k, (t_v[k, 0, s], t_v[k, 1, s]))
             finish_gradient(k)
 
+            @pl.when(k >= 2)
+            def _():
+                mix(k - 2)
+
     last = nk - 1
     arrived(last)
     send_gradient(last)
@@ -186,16 +215,19 @@
         p_send[j] = (acc[s] + product(last, (t_v[last, 0, s], t_v[last, 1, s]))).astype(BF16)
         p_copy(j).start()
     finish_gradient(last)
+    for k in range(max(0, nk - 3), last):
+        mix(k)
     total = acc[z] + product(last, (t_v[last, 0, z], t_v[last, 1, z]))
     for j in range(len(peers)):
         p_copy(j).wait_recv()
         total = total + p_recv[j].astype(F32)
     p_send[len(peers)] = total.astype(BF16)
-    p_store = pltpu.make_async_copy(p_send.at[len(peers)], p_out, store_sem.at[nk])
+    p_store = pltpu.make_async_copy(p_send.at[len(peers)], p_out, store_sem.at[nk, 0])
     p_store.start()
+    mix(last)
 
     for j in range(len(peers)):
-        cot_copy(j).wait_send()
+        cot_copy(j + 1).wait_send()
         p_copy(j).wait_send()
         for k in range(nk):
             for half in range(CORES):
@@ -203,9 +235,10 @@
     cur_copy.wait_send()
     for k in range(nk):
         gp_copy(k).wait_send()
-        s_copy(k).wait()
-        g_store(k).wait()
-    w_copy.wait()
+        s_copy(k).wait_send()
+        for i in range(3):
+            store(k, i).wait()
+    w_store.wait()
     p_store.wait()
 
 
@@ -222,11 +255,12 @@
         out_shape=(
             jax.ShapeDtypeStruct((own_tok, kv), BF16),
             jax.ShapeDtypeStruct((rows, kv), F32),
-            jax.ShapeDtypeStruct((rows, kv), BF16),
             jax.ShapeDtypeStruct((8, 128), F32),
+            jax.ShapeDtypeStruct((rows, kv), F32),
+            jax.ShapeDtypeStruct((rows, kv), F32),
         ),
         in_specs=[any_spec] * 4 + [pl.BlockSpec(memory_space=pltpu.SMEM)],
-        out_specs=[any_spec] * 4,
+        out_specs=[any_spec] * 5,
         scratch_shapes=[
             pltpu.VMEM((nk, CORES, chips, own_tok, width), BF16),
             pltpu.VMEM((chips, own_tok, kv), BF16),
@@ -240,10 +274,13 @@
             pltpu.VMEM((nk, width, kv), BF16),
             pltpu.VMEM((nk, width, kv), F32),
             pltpu.VMEM((nk, width, kv), BF16),
+            pltpu.VMEM((nk, width, kv), BF16),
+            pltpu.VMEM((rows, kv), F32),
             pltpu.VMEM((8, 128), F32),
-            dma((3,)), dma((nk, CORES)), dma((n,)), dma((n,)), dma((nk, CORES, n)), dma((nk, CORES, n)),
+            pltpu.VMEM((8, 128), F32),
+            dma((3,)), dma((nk, CORES)), dma((chips,)), dma((chips,)), dma((nk, CORES, n)), dma((nk, CORES, n)),
             dma(()), dma(()), dma((nk,)), dma((nk,)), dma((nk,)), dma((nk,)), dma((n,)), dma((n,)),
-            dma(()), dma(()), dma((nk + 1,)),
+            dma(()), dma(()), dma((nk + 1, 3)),
         ],
         compiler_params=pltpu.CompilerParams(
             collective_id=level, has_side_effects=True, vmem_limit_bytes=48 * 1024 * 1024),
@@ -253,20 +290,41 @@
     )(tokens, cotangent, numer, moment, weight)
 
 
+def hand_out_kernel(p, mix, w, vel, deb, p_out, mix_out, w_out, vel_out, deb_out, w_v, sem):
+    copies = [
+        pltpu.make_async_copy(made, out, sem.at[i])
+        for i, (made, out) in enumerate(((w, w_v), (mix, mix_out), (vel, vel_out), (deb, deb_out), (p, p_out)))
+    ]
+    for copy in copies:
+        copy.start()
+    copies[0].wait()
+    w_out[0] = jnp.max(w_v[...])
+    for copy in copies[1:]:
+        copy.wait()
+
+
+def hand_out(p, mix, w, vel, deb):
+    any_spec = pl.BlockSpec(memory_space=pl.ANY)
+    hbm = pl.BlockSpec(memory_space=pltpu.HBM)
+    like = lambda a: jax.ShapeDtypeStruct(a.shape, a.dtype)
+    return pl.pallas_call(
+        hand_out_kernel,
+        out_shape=(like(p), like(mix), jax.ShapeDtypeStruct((1,), F32), like(vel), like(deb)),
+        in_specs=[any_spec] * 5,
+        out_specs=[hbm, hbm, pl.BlockSpec(memory_space=pltpu.SMEM), hbm, hbm],
+        scratch_shapes=[pltpu.VMEM((8, 128), F32), pltpu.SemaphoreType.DMA((5,))],
+        cost_estimate=pl.CostEstimate(flops=0, bytes_accessed=12 * mix.size, transcendentals=0),
+        name="hand_out",
+    )(p, mix, w, vel, deb)
+
+
 def shards(tokens, cotangent, biased, momentum, weight, round_index):
     hops = lax.axis_size("replica").bit_length() - 1
     chips = lax.axis_size("shard") // CORES
     power = round_index[0] % hops
-    numer = biased[0]
-    moment = momentum[0]
     branches = [partial(push_call, level, chips) for level in range(hops)]
-    output, gradient, stepped_from, weight_from = lax.switch(
-        power, branches, tokens, cotangent, numer, moment, weight)
-    velocity = MOMENT * moment + gradient
-    stepped = numer - LEARN * (gradient + MOMENT * velocity)
-    mixed = 0.5 * (stepped + stepped_from.astype(F32))
-    weight_out = 0.5 * (weight + weight_from[0, :1])
-    debiased = mixed / weight_out[0]
+    made = lax.switch(power, branches, tokens, cotangent, biased[0], momentum[0], weight)
+    output, mixed, weight_out, velocity, debiased = hand_out(*made)
     return (output, mixed[None], weight_out, velocity[None], debiased[None])
 
 

time: 87.5 us -> 206 us (2.35)
  Pallas kernels: 76.8 us -> 205 us
  other arithmetic: 6.08 us -> 0 us
  between operations: 3.73 us -> 1.3 us
    pallas_call x0 -> x1, Pallas kernels: none -> 129 us  [hand_out(): pl.pallas_call(hand_out_kernel, out_shape=(like(p), like(mix), jax.ShapeD...]
    broadcast_in_dim x1 -> x0, other arithmetic: 6.08 us -> none  [shards(): return (output, mixed[None], weight_out, velocity[None], debiased[None])]
where the time goes in v2:
time: 206 us
  Pallas kernels  205 us (100%)
    pallas_call x1, Pallas kernels, hand_out(): pl.pallas_call(hand_out_kernel, out_shape=(like(p), like(mix), jax.ShapeD...  129 us
    pallas_call x1, Pallas kernels, push_call(): pl.pallas_call(partial(push_kernel, 1 << level, chips, nk), out_shape=(ja...  76.2 us

profile of v2, /device:TPU:17, one launch (start us, length us, event | category | flops | bytes accessed | tf_op | source)
XLA Modules:
  0.0 206.3 jit_solution(7268593053043004270)
XLA Ops:
  1.3 76.2 %conditional.1 = ((bf16[128,512]{1,0:T(8,128)(2,1)S(1)}, f32[1024,512]{1,0:T(8,128)S(1)}, f32[8,128]{1,0:T(8,128)S(1)}, f32[1024,512]{1,0:T(8,128)}, f32[1024,512]{1,0:T(8,128)})) conditional(s32[]{:T(128)} %clamp.3, (bf16[128,8192]{1,0:T(8,128)(2,1)}, bf16[128,512]{1,0:T(8,128)(2,1)}, f32[1024,512]{1,0:T(8,128)}, f32[1024,512]{1,0:T(8,128)}, ...), branch_computations={%region_0.1_spmd, %region_1.2_spmd} | conditional | flops 2147483648 | bytes 6291464 | solution.py:326
  1.3 76.2 %push_round_1.1 = (bf16[128,512]{1,0:T(8,128)(2,1)S(1)}, f32[1024,512]{1,0:T(8,128)S(1)}, f32[8,128]{1,0:T(8,128)S(1)}, f32[1024,512]{1,0:T(8,128)}, f32[1024,512]{1,0:T(8,128)}) custom-call(bf16[128,8192]{1,0:T(8,128)(2,1)} %get-tuple-element.25.tok, bf16[128,512]{1,0:T(8,128)(2,1)} %get-tuple-element.26.cot, f32[1024,512]{1,0:T(8,128)} %get-tuple-element.27.biased, ...), custom_call_target="tpu_custom_call" | custom-call | flops 2147483648 | bytes 6291456 | tf_op jit(solution)/shard_map/cond/branch_1_fun/push_round_1/pallas_call | solution.py:253
  77.5 128.7 %hand_out.1 = (bf16[128,512]{1,0:T(8,128)(2,1)}, f32[1024,512]{1,0:T(8,128)}, f32[1]{0:T(128)}, f32[1024,512]{1,0:T(8,128)}, f32[1024,512]{1,0:T(8,128)}) custom-call(bf16[128,512]{1,0:T(8,128)(2,1)S(1)} %get-tuple-element.45.p, f32[1024,512]{1,0:T(8,128)S(1)} %get-tuple-element.46.mix, f32[8,128]{1,0:T(8,128)S(1)} %get-tuple-element.47.w, ...), custom_call_target="tpu_custom_call" | custom-call | bytes 6291456 | tf_op jit(solution)/shard_map/hand_out/pallas_call | solution.py:310

commit v3 on v2

--- a/solution.py
+++ b/solution.py
@@ -31,15 +31,18 @@
     return order
 
 
-def push_kernel(dist, chips, nk, tok, cot, biased, momentum, weight,
+def push_kernel(dist, chips, nk, look, tok, cot, biased, momentum, weight,
                 p_out, mix_out, w_out, vel_out, deb_out,
                 t_v, c_v, b_v, m_v, cur, acc, p_send, p_recv, gp_send, gp_recv, g_v, s_send, s_recv, deb_v,
                 w_send, w_recv,
-                load_sem, own_sem, c_ssem, c_rsem, t_ssem, t_rsem, cur_ssem, cur_rsem,
+                load_sem, own_sem, c_ssem, c_rsem, t_ssem, t_rsem, e_ssem, e_rsem, cur_ssem, cur_rsem,
                 gp_ssem, gp_rsem, s_ssem, s_rsem, p_ssem, p_rsem, w_ssem, w_rsem, store_sem):
     rows, kv = b_v.shape
     own_tok = tok.shape[0]
     width = rows // nk
+    last = nk - 1
+    nt, block = p_send.shape[1], p_send.shape[2]
+    early = min(2, last)
     rep_tok = own_tok * chips * CORES
     replicas = lax.axis_size("replica")
     rep = lax.axis_index("replica")
@@ -73,6 +76,24 @@
             send_sem=t_ssem.at[k, half, j], recv_sem=t_rsem.at[k, half, j],
             device_id={"shard": peers[j] * CORES + c}, device_id_type=MESH)
 
+    def end_copy(t, half, j):
+        part = pl.ds(t * block, block)
+        return pltpu.make_async_remote_copy(
+            src_ref=tok.at[part, columns(peers[j], half, last)], dst_ref=t_v.at[last, half, z, part],
+            send_sem=e_ssem.at[t, half, j], recv_sem=e_rsem.at[t, half, j],
+            device_id={"shard": peers[j] * CORES + c}, device_id_type=MESH)
+
+    def send_chunk(k):
+        for j in range(len(peers)):
+            for half in range(CORES):
+                tok_copy(k, half, j).start()
+
+    def send_last():
+        for t in range(nt):
+            for j in range(len(peers)):
+                for half in range(CORES):
+                    end_copy(t, half, j).start()
+
     def cot_copy(x):
         low = x & -x
         held = z if x == low else flipped(z, x - low, chips)
@@ -80,10 +101,10 @@
             src_ref=c_v.at[held], dst_ref=c_v.at[held], send_sem=c_ssem.at[x], recv_sem=c_rsem.at[x],
             device_id={"shard": flipped(z, low, chips) * CORES + c}, device_id_type=MESH)
 
-    def p_copy(j):
-        return pltpu.make_async_remote_copy(
-            src_ref=p_send.at[j], dst_ref=p_recv.at[j], send_sem=p_ssem.at[j], recv_sem=p_rsem.at[j],
-            device_id={"shard": peers[j] * CORES + c}, device_id_type=MESH)
+    def p_copy(x, t):
+        return pltpu.make_async_remote_copy(
+            src_ref=p_send.at[x, t], dst_ref=p_recv.at[x, t], send_sem=p_ssem.at[x, t], recv_sem=p_rsem.at[x, t],
+            device_id={"shard": flipped(z, x & -x, chips) * CORES + c}, device_id_type=MESH)
 
     def gp_copy(k):
         return pltpu.make_async_remote_copy(
@@ -114,10 +135,8 @@
 
     loads[2].wait()
     cot_copy(chips // 2).start()
-    for k in range(nk):
-        for j in range(len(peers)):
-            for half in range(CORES):
-                tok_copy(k, half, j).start()
+    for k in range(early):
+        send_chunk(k)
 
     w_send[...] = jnp.full(w_send.shape, weight[0], F32)
     w_copy = pltpu.make_async_remote_copy(
@@ -133,7 +152,6 @@
         device_id={"shard": mate}, device_id_type=MESH)
     cur_copy.start()
     acc[...] = jnp.zeros(acc.shape, F32)
-    loads[1].wait()
     bit = chips // 4
     while bit >= 1:
         for x in range(2 * bit, chips, 4 * bit):
@@ -141,6 +159,11 @@
         for x in range(bit, chips, 2 * bit):
             cot_copy(x).start()
         bit //= 2
+    for k in range(early, min(look, last)):
+        send_chunk(k)
+    if look >= last:
+        send_last()
+    loads[1].wait()
     for x in range(1, chips, 2):
         cot_copy(x).wait_recv()
     cur_copy.wait_recv()
@@ -167,6 +190,37 @@
         here = pl.ds(pl.multiple_of(k * width, width), width)
         return (jnp.dot(t[0], cur[0, here, :], preferred_element_type=F32)
                 + jnp.dot(t[1], cur[1, here, :], preferred_element_type=F32))
+
+    def accumulate(k):
+        made = product(k, [t_v[k, half].reshape(chips * own_tok, width) for half in range(CORES)])
+        acc[...] += made.reshape(acc.shape)
+
+    def send_sums(bit, t):
+        part = pl.ds(t * block, block)
+        for x in range(bit, chips, 2 * bit):
+            p_send[x, t] = acc[flipped(z, x, chips), part, :].astype(BF16)
+            p_copy(x, t).start()
+
+    def add_sums(bit, t):
+        part = pl.ds(t * block, block)
+        for x in range(bit, chips, 2 * bit):
+            p_copy(x, t).wait_recv()
+            acc[flipped(z, x - bit, chips), part, :] += p_recv[x, t].astype(F32)
+
+    bits = [1 << i for i in range(chips.bit_length() - 1)]
+
+    def reduce_step(i, t):
+        part = pl.ds(t * block, block)
+        if i == 0:
+            made = product(last, [
+                t_v[last, half, :, part, :].reshape(chips * block, width) for half in range(CORES)])
+            acc[:, part, :] += made.reshape(chips, block, kv)
+        else:
+            add_sums(bits[i - 1], t)
+        if i < len(bits):
+            send_sums(bits[i], t)
+        else:
+            p_send[0, t] = acc[z, part, :].astype(BF16)
 
     def send_gradient(k):
         gp_send[k] = partial_gradient(k, other).astype(BF16)
@@ -195,43 +249,63 @@
         store(k, 2).start()
 
     if nk > 1:
-        @pl.loop(0, nk - 1)
+        @pl.loop(0, last)
         def _(k):
             arrived(k)
+
+            @pl.when(k + look < last)
+            def _():
+                send_chunk(k + look)
+
+            @pl.when(k + look == last)
+            def _():
+                send_last()
+
             send_gradient(k)
-            for s in range(chips):
-                acc[s] += product(k, (t_v[k, 0, s], t_v[k, 1, s]))
+            accumulate(k)
             finish_gradient(k)
 
             @pl.when(k >= 2)
             def _():
                 mix(k - 2)
 
-    last = nk - 1
-    arrived(last)
-    send_gradient(last)
-    for j in range(len(peers)):
-        s = peers[j]
-        p_send[j] = (acc[s] + product(last, (t_v[last, 0, s], t_v[last, 1, s]))).astype(BF16)
-        p_copy(j).start()
+    for half in range(CORES):
+        own_copy(last, half).wait()
+    for t in range(nt):
+        for j in range(len(peers)):
+            for half in range(CORES):
+                end_copy(t, half, j).wait_recv()
+        reduce_step(0, t)
+        if t == nt - 1:
+            send_gradient(last)
+        for i in range(1, len(bits) + 1):
+            if t >= i:
+                reduce_step(i, t - i)
     finish_gradient(last)
     for k in range(max(0, nk - 3), last):
         mix(k)
-    total = acc[z] + product(last, (t_v[last, 0, z], t_v[last, 1, z]))
+    for late in range(nt, nt + len(bits)):
+        for i in range(1, len(bits) + 1):
+            if 0 <= late - i < nt:
+                reduce_step(i, late - i)
+    p_stores = [
+        pltpu.make_async_copy(p_send.at[0, t], p_out.at[pl.ds(t * block, block), :], p_ssem.at[0, t])
+        for t in range(nt)
+    ]
+    for p_store in p_stores:
+        p_store.start()
+    mix(last)
+
+    for x in range(1, chips):
+        cot_copy(x).wait_send()
+        for t in range(nt):
+            p_copy(x, t).wait_send()
     for j in range(len(peers)):
-        p_copy(j).wait_recv()
-        total = total + p_recv[j].astype(F32)
-    p_send[len(peers)] = total.astype(BF16)
-    p_store = pltpu.make_async_copy(p_send.at[len(peers)], p_out, store_sem.at[nk, 0])
-    p_store.start()
-    mix(last)
-
-    for j in range(len(peers)):
-        cot_copy(j + 1).wait_send()
-        p_copy(j).wait_send()
-        for k in range(nk):
-            for half in range(CORES):
+        for half in range(CORES):
+            for k in range(last):
                 tok_copy(k, half, j).wait_send()
+            for t in range(nt):
+                end_copy(t, half, j).wait_send()
     cur_copy.wait_send()
     for k in range(nk):
         gp_copy(k).wait_send()
@@ -239,19 +313,22 @@
         for i in range(3):
             store(k, i).wait()
     w_store.wait()
-    p_store.wait()
+    for p_store in p_stores:
+        p_store.wait()
 
 
 def push_call(level, chips, tokens, cotangent, numer, moment, weight):
     own_tok, features = tokens.shape
     rows, kv = numer.shape
-    nk = max(1, rows // 256)
+    nk = max(1, rows // 128)
+    nt = max(1, own_tok // 32)
+    block = own_tok // nt
     width = rows // nk
     n = chips - 1
     any_spec = pl.BlockSpec(memory_space=pl.ANY)
     dma = pltpu.SemaphoreType.DMA
     return pl.pallas_call(
-        partial(push_kernel, 1 << level, chips, nk),
+        partial(push_kernel, 1 << level, chips, nk, 5),
         out_shape=(
             jax.ShapeDtypeStruct((own_tok, kv), BF16),
             jax.ShapeDtypeStruct((rows, kv), F32),
@@ -268,8 +345,8 @@
             pltpu.VMEM((rows, kv), F32),
             pltpu.VMEM((CORES, rows, kv), BF16),
             pltpu.VMEM((chips, own_tok, kv), F32),
-            pltpu.VMEM((chips, own_tok, kv), BF16),
-            pltpu.VMEM((n, own_tok, kv), BF16),
+            pltpu.VMEM((chips, nt, block, kv), BF16),
+            pltpu.VMEM((chips, nt, block, kv), BF16),
             pltpu.VMEM((nk, width, kv), BF16),
             pltpu.VMEM((nk, width, kv), BF16),
             pltpu.VMEM((nk, width, kv), F32),
@@ -279,11 +356,12 @@
             pltpu.VMEM((8, 128), F32),
             pltpu.VMEM((8, 128), F32),
             dma((3,)), dma((nk, CORES)), dma((chips,)), dma((chips,)), dma((nk, CORES, n)), dma((nk, CORES, n)),
-            dma(()), dma(()), dma((nk,)), dma((nk,)), dma((nk,)), dma((nk,)), dma((n,)), dma((n,)),
-            dma(()), dma(()), dma((nk + 1, 3)),
+            dma((nt, CORES, n)), dma((nt, CORES, n)),
+            dma(()), dma(()), dma((nk,)), dma((nk,)), dma((nk,)), dma((nk,)), dma((chips, nt)), dma((chips, nt)),
+            dma(()), dma(()), dma((nk, 3)),
         ],
         compiler_params=pltpu.CompilerParams(
-            collective_id=level, has_side_effects=True, vmem_limit_bytes=48 * 1024 * 1024),
+            collective_id=level, has_side_effects=True, vmem_limit_bytes=32 * 1024 * 1024),
         cost_estimate=pl.CostEstimate(
             flops=4 * own_tok * features * kv, bytes_accessed=12 * rows * kv, transcendentals=0),
         name=f"push_round_{level}",

time: 206 us -> 206 us (level)
  the two profiles are of different devices: /device:TPU:17 before, /device:TPU:0 now
where the time goes in v3:
time: 206 us; the launch traced here: 205 us
  Pallas kernels  204 us (99%)
    pallas_call x1, Pallas kernels, hand_out(): pl.pallas_call(hand_out_kernel, out_shape=(like(p), like(mix), jax.ShapeD...  129 us
    pallas_call x1, Pallas kernels, push_call(): pl.pallas_call(partial(push_kernel, 1 << level, chips, nk, 5), out_shape=...  75.2 us

profile of v3, /device:TPU:0, one launch (start us, length us, event | category | flops | bytes accessed | tf_op | source)
XLA Modules:
  0.0 205.2 jit_solution(11808095240015285416)
XLA Ops:
  1.3 75.2 %conditional.1 = ((bf16[128,512]{1,0:T(8,128)(2,1)S(1)}, f32[1024,512]{1,0:T(8,128)S(1)}, f32[8,128]{1,0:T(8,128)S(1)}, f32[1024,512]{1,0:T(8,128)}, f32[1024,512]{1,0:T(8,128)})) conditional(s32[]{:T(128)} %clamp.3, (bf16[128,8192]{1,0:T(8,128)(2,1)}, bf16[128,512]{1,0:T(8,128)(2,1)}, f32[1024,512]{1,0:T(8,128)}, f32[1024,512]{1,0:T(8,128)}, ...), branch_computations={%region_0.1_spmd, %region_1.2_spmd} | conditional | flops 2147483648 | bytes 6291464 | solution.py:404
  1.3 75.2 %push_round_1.1 = (bf16[128,512]{1,0:T(8,128)(2,1)S(1)}, f32[1024,512]{1,0:T(8,128)S(1)}, f32[8,128]{1,0:T(8,128)S(1)}, f32[1024,512]{1,0:T(8,128)}, f32[1024,512]{1,0:T(8,128)}) custom-call(bf16[128,8192]{1,0:T(8,128)(2,1)} %get-tuple-element.25.tok, bf16[128,512]{1,0:T(8,128)(2,1)} %get-tuple-element.26.cot, f32[1024,512]{1,0:T(8,128)} %get-tuple-element.27.biased, ...), custom_call_target="tpu_custom_call" | custom-call | flops 2147483648 | bytes 6291456 | tf_op jit(solution)/shard_map/cond/branch_1_fun/push_round_1/pallas_call | solution.py:330
  76.5 128.7 %hand_out.1 = (bf16[128,512]{1,0:T(8,128)(2,1)}, f32[1024,512]{1,0:T(8,128)}, f32[1]{0:T(128)}, f32[1024,512]{1,0:T(8,128)}, f32[1024,512]{1,0:T(8,128)}) custom-call(bf16[128,512]{1,0:T(8,128)(2,1)S(1)} %get-tuple-element.45.p, f32[1024,512]{1,0:T(8,128)S(1)} %get-tuple-element.46.mix, f32[8,128]{1,0:T(8,128)S(1)} %get-tuple-element.47.w, ...), custom_call_target="tpu_custom_call" | custom-call | bytes 6291456 | tf_op jit(solution)/shard_map/hand_out/pallas_call | solution.py:388

commit v4 on v3

--- a/solution.py
+++ b/solution.py
@@ -33,7 +33,7 @@
 
 def push_kernel(dist, chips, nk, look, tok, cot, biased, momentum, weight,
                 p_out, mix_out, w_out, vel_out, deb_out,
-                t_v, c_v, b_v, m_v, cur, acc, p_send, p_recv, gp_send, gp_recv, g_v, s_send, s_recv, deb_v,
+                tok_v, t_v, c_v, b_v, m_v, cur, acc, p_send, p_recv, gp_send, gp_recv, g_v, s_send, s_recv, deb_v,
                 w_send, w_recv,
                 load_sem, own_sem, c_ssem, c_rsem, t_ssem, t_rsem, e_ssem, e_rsem, cur_ssem, cur_rsem,
                 gp_ssem, gp_rsem, s_ssem, s_rsem, p_ssem, p_rsem, w_ssem, w_rsem, store_sem):
@@ -60,8 +60,9 @@
         pltpu.make_async_copy(biased, b_v, load_sem.at[0]),
         pltpu.make_async_copy(momentum, m_v, load_sem.at[1]),
         pltpu.make_async_copy(cot, c_v.at[z], load_sem.at[2]),
+        pltpu.make_async_copy(tok, tok_v, load_sem.at[3]),
     ]
-    for load in loads:
+    for load in loads[::-1]:
         load.start()
 
     def columns(chip, half, k):
@@ -72,14 +73,14 @@
 
     def tok_copy(k, half, j):
         return pltpu.make_async_remote_copy(
-            src_ref=tok.at[:, columns(peers[j], half, k)], dst_ref=t_v.at[k, half, z],
+            src_ref=tok_v.at[:, columns(peers[j], half, k)], dst_ref=t_v.at[k, half, z],
             send_sem=t_ssem.at[k, half, j], recv_sem=t_rsem.at[k, half, j],
             device_id={"shard": peers[j] * CORES + c}, device_id_type=MESH)
 
     def end_copy(t, half, j):
         part = pl.ds(t * block, block)
         return pltpu.make_async_remote_copy(
-            src_ref=tok.at[part, columns(peers[j], half, last)], dst_ref=t_v.at[last, half, z, part],
+            src_ref=tok_v.at[part, columns(peers[j], half, last)], dst_ref=t_v.at[last, half, z, part],
             send_sem=e_ssem.at[t, half, j], recv_sem=e_rsem.at[t, half, j],
             device_id={"shard": peers[j] * CORES + c}, device_id_type=MESH)
 
@@ -135,6 +136,7 @@
 
     loads[2].wait()
     cot_copy(chips // 2).start()
+    loads[3].wait()
     for k in range(early):
         send_chunk(k)
 
@@ -339,6 +341,7 @@
         in_specs=[any_spec] * 4 + [pl.BlockSpec(memory_space=pltpu.SMEM)],
         out_specs=[any_spec] * 5,
         scratch_shapes=[
+            pltpu.VMEM((own_tok, features), BF16),
             pltpu.VMEM((nk, CORES, chips, own_tok, width), BF16),
             pltpu.VMEM((chips, own_tok, kv), BF16),
             pltpu.VMEM((rows, kv), F32),
@@ -355,7 +358,7 @@
             pltpu.VMEM((rows, kv), F32),
             pltpu.VMEM((8, 128), F32),
             pltpu.VMEM((8, 128), F32),
-            dma((3,)), dma((nk, CORES)), dma((chips,)), dma((chips,)), dma((nk, CORES, n)), dma((nk, CORES, n)),
+            dma((4,)), dma((nk, CORES)), dma((chips,)), dma((chips,)), dma((nk, CORES, n)), dma((nk, CORES, n)),
             dma((nt, CORES, n)), dma((nt, CORES, n)),
             dma(()), dma(()), dma((nk,)), dma((nk,)), dma((nk,)), dma((nk,)), dma((chips, nt)), dma((chips, nt)),
             dma(()), dma(()), dma((nk, 3)),
@@ -391,6 +394,7 @@
         in_specs=[any_spec] * 5,
         out_specs=[hbm, hbm, pl.BlockSpec(memory_space=pltpu.SMEM), hbm, hbm],
         scratch_shapes=[pltpu.VMEM((8, 128), F32), pltpu.SemaphoreType.DMA((5,))],
+        compiler_params=pltpu.CompilerParams(vmem_limit_bytes=1024 * 1024),
         cost_estimate=pl.CostEstimate(flops=0, bytes_accessed=12 * mix.size, transcendentals=0),
         name="hand_out",
     )(p, mix, w, vel, deb)

time: 206 us -> 205 us (level)
  no operation moved by 1% of the time
where the time goes in v4:
time: 205 us
  Pallas kernels  204 us (100%)
    pallas_call x1, Pallas kernels, hand_out(): pl.pallas_call(hand_out_kernel, out_shape=(like(p), like(mix), jax.ShapeD...  129 us
    pallas_call x1, Pallas kernels, push_call(): pl.pallas_call(partial(push_kernel, 1 << level, chips, nk, 5), out_shape=...  75 us

profile of v4, /device:TPU:0, one launch (start us, length us, event | category | flops | bytes accessed | tf_op | source)
XLA Modules:
  0.0 205.0 jit_solution(1351758681213467973)
XLA Ops:
  1.3 75.0 %conditional.1 = ((bf16[128,512]{1,0:T(8,128)(2,1)S(1)}, f32[1024,512]{1,0:T(8,128)S(1)}, f32[8,128]{1,0:T(8,128)S(1)}, f32[1024,512]{1,0:T(8,128)}, f32[1024,512]{1,0:T(8,128)})) conditional(s32[]{:T(128)} %clamp.3, (bf16[128,8192]{1,0:T(8,128)(2,1)}, bf16[128,512]{1,0:T(8,128)(2,1)}, f32[1024,512]{1,0:T(8,128)}, f32[1024,512]{1,0:T(8,128)}, ...), branch_computations={%region_0.1_spmd, %region_1.2_spmd} | conditional | flops 2147483648 | bytes 6291464 | solution.py:408
  1.3 75.0 %push_round_0.1 = (bf16[128,512]{1,0:T(8,128)(2,1)S(1)}, f32[1024,512]{1,0:T(8,128)S(1)}, f32[8,128]{1,0:T(8,128)S(1)}, f32[1024,512]{1,0:T(8,128)}, f32[1024,512]{1,0:T(8,128)}) custom-call(bf16[128,8192]{1,0:T(8,128)(2,1)} %get-tuple-element.20.tok, bf16[128,512]{1,0:T(8,128)(2,1)} %get-tuple-element.21.cot, f32[1024,512]{1,0:T(8,128)} %get-tuple-element.22.biased, ...), custom_call_target="tpu_custom_call" | custom-call | flops 2147483648 | bytes 6291456 | tf_op jit(solution)/shard_map/cond/branch_0_fun/push_round_0/pallas_call | solution.py:332
  76.3 128.7 %hand_out.1 = (bf16[128,512]{1,0:T(8,128)(2,1)}, f32[1024,512]{1,0:T(8,128)}, f32[1]{0:T(128)}, f32[1024,512]{1,0:T(8,128)}, f32[1024,512]{1,0:T(8,128)}) custom-call(bf16[128,512]{1,0:T(8,128)(2,1)S(1)} %get-tuple-element.45.p, f32[1024,512]{1,0:T(8,128)S(1)} %get-tuple-element.46.mix, f32[8,128]{1,0:T(8,128)S(1)} %get-tuple-element.47.w, ...), custom_call_target="tpu_custom_call" | custom-call | bytes 6291456 | tf_op jit(solution)/shard_map/hand_out/pallas_call | solution.py:391

commit v5 on v4

--- a/solution.py
+++ b/solution.py
@@ -32,8 +32,8 @@
 
 
 def push_kernel(dist, chips, nk, look, tok, cot, biased, momentum, weight,
-                p_out, mix_out, w_out, vel_out, deb_out,
-                tok_v, t_v, c_v, b_v, m_v, cur, acc, p_send, p_recv, gp_send, gp_recv, g_v, s_send, s_recv, deb_v,
+                p_out, mix_out, w_out, vel_out,
+                tok_v, t_v, c_v, b_v, m_v, cur, acc, p_send, p_recv, gp_send, gp_recv, g_v, s_send, s_recv,
                 w_send, w_recv,
                 load_sem, own_sem, c_ssem, c_rsem, t_ssem, t_rsem, e_ssem, e_rsem, cur_ssem, cur_rsem,
                 gp_ssem, gp_rsem, s_ssem, s_rsem, p_ssem, p_rsem, w_ssem, w_rsem, store_sem):
@@ -120,24 +120,28 @@
 
     def store(k, i):
         here = pl.ds(pl.multiple_of(k * width, width), width)
-        made, out = ((m_v, vel_out), (b_v, mix_out), (deb_v, deb_out))[i]
+        made, out = ((m_v, vel_out), (b_v, mix_out))[i]
         return pltpu.make_async_copy(made.at[here, :], out.at[here, :], store_sem.at[k, i])
 
     for k in range(nk):
         for half in range(CORES):
             own_copy(k, half).start()
 
+    mine = cur.at[c]
     barrier = pltpu.get_barrier_semaphore()
     for peer in peers:
         pl.semaphore_signal(barrier, inc=1, device_id={"shard": peer * CORES + c}, device_id_type=MESH)
     pl.semaphore_signal(barrier, inc=1, device_id={"shard": mate}, device_id_type=MESH)
     pl.semaphore_signal(barrier, inc=1, device_id={"replica": behind}, device_id_type=MESH)
+    loads[0].wait()
+    mine[...] = (b_v[...] / weight[0]).astype(BF16)
+    acc[...] = jnp.zeros(acc.shape, F32)
     pl.semaphore_wait(barrier, len(peers) + 2)
 
     loads[2].wait()
     cot_copy(chips // 2).start()
     loads[3].wait()
-    for k in range(early):
+    for k in range(min(1, last)):
         send_chunk(k)
 
     w_send[...] = jnp.full(w_send.shape, weight[0], F32)
@@ -146,14 +150,12 @@
         device_id={"replica": ahead}, device_id_type=MESH)
     w_copy.start()
 
-    loads[0].wait()
-    mine = cur.at[c]
-    mine[...] = (b_v[...] / weight[0]).astype(BF16)
     cur_copy = pltpu.make_async_remote_copy(
         src_ref=mine, dst_ref=mine, send_sem=cur_ssem, recv_sem=cur_rsem,
         device_id={"shard": mate}, device_id_type=MESH)
     cur_copy.start()
-    acc[...] = jnp.zeros(acc.shape, F32)
+    for k in range(min(1, last), early):
+        send_chunk(k)
     bit = chips // 4
     while bit >= 1:
         for x in range(2 * bit, chips, 4 * bit):
@@ -227,7 +229,6 @@
     def send_gradient(k):
         gp_send[k] = partial_gradient(k, other).astype(BF16)
         gp_copy(k).start()
-        g_v[k] = partial_gradient(k, c)
 
     def finish_gradient(k):
         here = pl.ds(pl.multiple_of(k * width, width), width)
@@ -244,16 +245,14 @@
     def mix(k):
         here = pl.ds(pl.multiple_of(k * width, width), width)
         s_copy(k).wait_recv()
-        mixed = 0.5 * (b_v[here, :] + s_recv[k].astype(F32))
-        b_v[here, :] = mixed
-        deb_v[here, :] = mixed / w_send[0:1, 0:1]
+        b_v[here, :] = 0.5 * (b_v[here, :] + s_recv[k].astype(F32))
         store(k, 1).start()
-        store(k, 2).start()
 
     if nk > 1:
         @pl.loop(0, last)
         def _(k):
             arrived(k)
+            send_gradient(k)
 
             @pl.when(k + look < last)
             def _():
@@ -263,13 +262,16 @@
             def _():
                 send_last()
 
-            send_gradient(k)
+            g_v[k] = partial_gradient(k, c)
             accumulate(k)
-            finish_gradient(k)
-
-            @pl.when(k >= 2)
+
+            @pl.when(k >= 1)
             def _():
-                mix(k - 2)
+                finish_gradient(k - 1)
+
+            @pl.when(k >= 4)
+            def _():
+                mix(k - 4)
 
     for half in range(CORES):
         own_copy(last, half).wait()
@@ -280,11 +282,14 @@
         reduce_step(0, t)
         if t == nt - 1:
             send_gradient(last)
+            if last >= 1:
+                finish_gradient(last - 1)
+            g_v[last] = partial_gradient(last, c)
         for i in range(1, len(bits) + 1):
             if t >= i:
                 reduce_step(i, t - i)
     finish_gradient(last)
-    for k in range(max(0, nk - 3), last):
+    for k in range(max(0, last - 4), last):
         mix(k)
     for late in range(nt, nt + len(bits)):
         for i in range(1, len(bits) + 1):
@@ -312,7 +317,7 @@
     for k in range(nk):
         gp_copy(k).wait_send()
         s_copy(k).wait_send()
-        for i in range(3):
+        for i in range(2):
             store(k, i).wait()
     w_store.wait()
     for p_store in p_stores:
@@ -330,16 +335,15 @@
     any_spec = pl.BlockSpec(memory_space=pl.ANY)
     dma = pltpu.SemaphoreType.DMA
     return pl.pallas_call(
-        partial(push_kernel, 1 << level, chips, nk, 5),
+        partial(push_kernel, 1 << level, chips, nk, 2),
         out_shape=(
             jax.ShapeDtypeStruct((own_tok, kv), BF16),
             jax.ShapeDtypeStruct((rows, kv), F32),
             jax.ShapeDtypeStruct((8, 128), F32),
             jax.ShapeDtypeStruct((rows, kv), F32),
-            jax.ShapeDtypeStruct((rows, kv), F32),
         ),
         in_specs=[any_spec] * 4 + [pl.BlockSpec(memory_space=pltpu.SMEM)],
-        out_specs=[any_spec] * 5,
+        out_specs=[any_spec] * 4,
         scratch_shapes=[
             pltpu.VMEM((own_tok, features), BF16),
             pltpu.VMEM((nk, CORES, chips, own_tok, width), BF16),
@@ -355,13 +359,12 @@
             pltpu.VMEM((nk, width, kv), F32),
             pltpu.VMEM((nk, width, kv), BF16),
             pltpu.VMEM((nk, width, kv), BF16),
-            pltpu.VMEM((rows, kv), F32),
             pltpu.VMEM((8, 128), F32),
             pltpu.VMEM((8, 128), F32),
             dma((4,)), dma((nk, CORES)), dma((chips,)), dma((chips,)), dma((nk, CORES, n)), dma((nk, CORES, n)),
             dma((nt, CORES, n)), dma((nt, CORES, n)),
             dma(()), dma(()), dma((nk,)), dma((nk,)), dma((nk,)), dma((nk,)), dma((chips, nt)), dma((chips, nt)),
-            dma(()), dma(()), dma((nk, 3)),
+            dma(()), dma(()), dma((nk, 2)),
         ],
         compiler_params=pltpu.CompilerParams(
             collective_id=level, has_side_effects=True, vmem_limit_bytes=32 * 1024 * 1024),
@@ -371,33 +374,65 @@
     )(tokens, cotangent, numer, moment, weight)
 
 
-def hand_out_kernel(p, mix, w, vel, deb, p_out, mix_out, w_out, vel_out, deb_out, w_v, sem):
-    copies = [
-        pltpu.make_async_copy(made, out, sem.at[i])
-        for i, (made, out) in enumerate(((w, w_v), (mix, mix_out), (vel, vel_out), (deb, deb_out), (p, p_out)))
-    ]
-    for copy in copies:
-        copy.start()
-    copies[0].wait()
+def hand_out_kernel(parts, p, mix, w, vel, p_out, mix_out, w_out, vel_out, deb_out,
+                    p_v, mix_v, w_v, vel_v, deb_v, in_sem, out_sem, small_sem):
+    size = mix_v.shape[0] // parts
+
+    def load(i, which):
+        here = pl.ds(i * size, size)
+        made, held = ((mix, mix_v), (vel, vel_v))[which]
+        return pltpu.make_async_copy(made.at[here, :], held.at[here, :], in_sem.at[i, which])
+
+    def store(i, which):
+        here = pl.ds(i * size, size)
+        held, out = ((mix_v, mix_out), (vel_v, vel_out), (deb_v, deb_out))[which]
+        return pltpu.make_async_copy(held.at[here, :], out.at[here, :], out_sem.at[i, which])
+
+    w_load = pltpu.make_async_copy(w, w_v, small_sem.at[0])
+    p_load = pltpu.make_async_copy(p, p_v, small_sem.at[1])
+    p_store = pltpu.make_async_copy(p_v, p_out, small_sem.at[2])
+    w_load.start()
+    for i in range(parts):
+        load(i, 0).start()
+        load(i, 1).start()
+    p_load.start()
+    w_load.wait()
+    scale = w_v[0:1, 0:1]
     w_out[0] = jnp.max(w_v[...])
-    for copy in copies[1:]:
-        copy.wait()
-
-
-def hand_out(p, mix, w, vel, deb):
+    for i in range(parts):
+        here = pl.ds(i * size, size)
+        load(i, 0).wait()
+        store(i, 0).start()
+        deb_v[here, :] = mix_v[here, :] / scale
+        store(i, 2).start()
+        load(i, 1).wait()
+        store(i, 1).start()
+    p_load.wait()
+    p_store.start()
+    for i in range(parts):
+        for which in range(3):
+            store(i, which).wait()
+    p_store.wait()
+
+
+def hand_out(p, mix, w, vel):
     any_spec = pl.BlockSpec(memory_space=pl.ANY)
     hbm = pl.BlockSpec(memory_space=pltpu.HBM)
     like = lambda a: jax.ShapeDtypeStruct(a.shape, a.dtype)
+    held = lambda a: pltpu.VMEM(a.shape, a.dtype)
+    parts = max(1, mix.shape[0] // 128)
+    dma = pltpu.SemaphoreType.DMA
     return pl.pallas_call(
-        hand_out_kernel,
-        out_shape=(like(p), like(mix), jax.ShapeDtypeStruct((1,), F32), like(vel), like(deb)),
-        in_specs=[any_spec] * 5,
+        partial(hand_out_kernel, parts),
+        out_shape=(like(p), like(mix), jax.ShapeDtypeStruct((1,), F32), like(vel), like(mix)),
+        in_specs=[any_spec] * 4,
         out_specs=[hbm, hbm, pl.BlockSpec(memory_space=pltpu.SMEM), hbm, hbm],
-        scratch_shapes=[pltpu.VMEM((8, 128), F32), pltpu.SemaphoreType.DMA((5,))],
-        compiler_params=pltpu.CompilerParams(vmem_limit_bytes=1024 * 1024),
+        scratch_shapes=[held(p), held(mix), held(w), held(vel), held(mix),
+                        dma((parts, 2)), dma((parts, 3)), dma((3,))],
+        compiler_params=pltpu.CompilerParams(vmem_limit_bytes=8 * 1024 * 1024),
         cost_estimate=pl.CostEstimate(flops=0, bytes_accessed=12 * mix.size, transcendentals=0),
         name="hand_out",
-    )(p, mix, w, vel, deb)
+    )(p, mix, w, vel)
 
 
 def shards(tokens, cotangent, biased, momentum, weight, round_index):

time: 205 us -> 85.9 us (0.42)
  Pallas kernels: 204 us -> 83.9 us
    pallas_call x2, Pallas kernels: 204 us -> 83.9 us  [the longest x1 79.6 us: push_call(): pl.pallas_call(partial(push_kernel, 1 << level, chips, nk, 2), out_shape=...]
where the time goes in v5:
time: 85.9 us; the launch traced here: 85.2 us
  Pallas kernels  83.9 us (98%)
  between operations  1.3 us (2%)
    pallas_call x1, Pallas kernels, push_call(): pl.pallas_call(partial(push_kernel, 1 << level, chips, nk, 2), out_shape=...  79.6 us
    pallas_call x1, Pallas kernels, hand_out(): pl.pallas_call(partial(hand_out_kernel, parts), out_shape=(like(p), like(...  4.36 us

profile of v5, /device:TPU:0, one launch (start us, length us, event | category | flops | bytes accessed | tf_op | source)
XLA Modules:
  0.0 85.2 jit_solution(376922871702259397)
XLA Ops:
  1.3 79.6 %conditional.1 = ((bf16[128,512]{1,0:T(8,128)(2,1)S(1)}, f32[1024,512]{1,0:T(8,128)S(1)}, f32[8,128]{1,0:T(8,128)S(1)}, f32[1024,512]{1,0:T(8,128)})) conditional(s32[]{:T(128)} %clamp.3, (bf16[128,8192]{1,0:T(8,128)(2,1)}, bf16[128,512]{1,0:T(8,128)(2,1)}, f32[1024,512]{1,0:T(8,128)}, f32[1024,512]{1,0:T(8,128)}, f32[1]{0:T(128)}) %tuple.22, ...), branch_computations={%region_0.1_spmd, %region_1.2_spmd} | conditional | flops 2147483648 | bytes 6291464 | solution.py:443
  1.3 79.6 %push_round_1.1 = (bf16[128,512]{1,0:T(8,128)(2,1)S(1)}, f32[1024,512]{1,0:T(8,128)S(1)}, f32[8,128]{1,0:T(8,128)S(1)}, f32[1024,512]{1,0:T(8,128)}) custom-call(bf16[128,8192]{1,0:T(8,128)(2,1)} %get-tuple-element.25.tok, bf16[128,512]{1,0:T(8,128)(2,1)} %get-tuple-element.26.cot, f32[1024,512]{1,0:T(8,128)} %get-tuple-element.27.biased, ...), custom_call_target="tpu_custom_call" | custom-call | flops 2147483648 | bytes 6291456 | tf_op jit(solution)/shard_map/cond/branch_1_fun/push_round_1/pallas_call | solution.py:337
  80.9 4.4 %hand_out.1 = (bf16[128,512]{1,0:T(8,128)(2,1)}, f32[1024,512]{1,0:T(8,128)}, f32[1]{0:T(128)}, f32[1024,512]{1,0:T(8,128)}, f32[1024,512]{1,0:T(8,128)}) custom-call(bf16[128,512]{1,0:T(8,128)(2,1)S(1)} %get-tuple-element.44.p, f32[1024,512]{1,0:T(8,128)S(1)} %get-tuple-element.45.mix, f32[8,128]{1,0:T(8,128)S(1)} %get-tuple-element.46.w, ...), custom_call_target="tpu_custom_call" | custom-call | bytes 6291456 | tf_op jit(solution)/shard_map/hand_out/pallas_call | solution.py:425

commit v6 on v5

--- a/solution.py
+++ b/solution.py
@@ -10,7 +10,7 @@
 MOMENT = 0.9
 LEARN = 0.5
 MESH = pl.DeviceIdType.MESH
-CORES = 2
+CORES = 1
 BF16 = jnp.bfloat16
 F32 = jnp.float32
 
@@ -33,10 +33,9 @@
 
 def push_kernel(dist, chips, nk, look, tok, cot, biased, momentum, weight,
                 p_out, mix_out, w_out, vel_out,
-                tok_v, t_v, c_v, b_v, m_v, cur, acc, p_send, p_recv, gp_send, gp_recv, g_v, s_send, s_recv,
+                tok_v, t_v, c_v, b_v, m_v, cur, acc, p_send, p_recv, s_send, s_recv,
                 w_send, w_recv,
-                load_sem, own_sem, c_ssem, c_rsem, t_ssem, t_rsem, e_ssem, e_rsem, cur_ssem, cur_rsem,
-                gp_ssem, gp_rsem, s_ssem, s_rsem, p_ssem, p_rsem, w_ssem, w_rsem, store_sem):
+                load_sem, own_sem, c_ssem, c_rsem, t_ssem, t_rsem, e_ssem, e_rsem, s_ssem, s_rsem, p_ssem, p_rsem, w_ssem, w_rsem, store_sem):
     rows, kv = b_v.shape
     own_tok = tok.shape[0]
     width = rows // nk
@@ -49,8 +48,6 @@
     shard = lax.axis_index("shard")
     z = shard // CORES
     c = shard % CORES
-    other = 1 - c
-    mate = z * CORES + other
     ahead = (rep + dist) % replicas
     behind = (rep + replicas - dist) % replicas
     order = partners(chips)
@@ -107,11 +104,6 @@
             src_ref=p_send.at[x, t], dst_ref=p_recv.at[x, t], send_sem=p_ssem.at[x, t], recv_sem=p_rsem.at[x, t],
             device_id={"shard": flipped(z, x & -x, chips) * CORES + c}, device_id_type=MESH)
 
-    def gp_copy(k):
-        return pltpu.make_async_remote_copy(
-            src_ref=gp_send.at[k], dst_ref=gp_recv.at[k], send_sem=gp_ssem.at[k], recv_sem=gp_rsem.at[k],
-            device_id={"shard": mate}, device_id_type=MESH)
-
     def s_copy(k):
         return pltpu.make_async_remote_copy(
             src_ref=s_send.at[k], dst_ref=s_recv.at[k],
@@ -131,12 +123,11 @@
     barrier = pltpu.get_barrier_semaphore()
     for peer in peers:
         pl.semaphore_signal(barrier, inc=1, device_id={"shard": peer * CORES + c}, device_id_type=MESH)
-    pl.semaphore_signal(barrier, inc=1, device_id={"shard": mate}, device_id_type=MESH)
     pl.semaphore_signal(barrier, inc=1, device_id={"replica": behind}, device_id_type=MESH)
     loads[0].wait()
     mine[...] = (b_v[...] / weight[0]).astype(BF16)
     acc[...] = jnp.zeros(acc.shape, F32)
-    pl.semaphore_wait(barrier, len(peers) + 2)
+    pl.semaphore_wait(barrier, len(peers) + 1)
 
     loads[2].wait()
     cot_copy(chips // 2).start()
@@ -150,27 +141,23 @@
         device_id={"replica": ahead}, device_id_type=MESH)
     w_copy.start()
 
-    cur_copy = pltpu.make_async_remote_copy(
-        src_ref=mine, dst_ref=mine, send_sem=cur_ssem, recv_sem=cur_rsem,
-        device_id={"shard": mate}, device_id_type=MESH)
-    cur_copy.start()
-    for k in range(min(1, last), early):
-        send_chunk(k)
-    bit = chips // 4
+    bit, sent = chips // 4, min(1, last)
     while bit >= 1:
         for x in range(2 * bit, chips, 4 * bit):
             cot_copy(x).wait_recv()
         for x in range(bit, chips, 2 * bit):
             cot_copy(x).start()
+        if sent < min(look, last):
+            send_chunk(sent)
+            sent += 1
         bit //= 2
-    for k in range(early, min(look, last)):
+    for k in range(sent, min(look, last)):
         send_chunk(k)
     if look >= last:
         send_last()
     loads[1].wait()
     for x in range(1, chips, 2):
         cot_copy(x).wait_recv()
-    cur_copy.wait_recv()
     w_copy.wait()
     w_send[...] = 0.5 * (w_send[...] + w_recv[...])
     w_store = pltpu.make_async_copy(w_send, w_out, w_ssem)
@@ -192,11 +179,10 @@
 
     def product(k, t):
         here = pl.ds(pl.multiple_of(k * width, width), width)
-        return (jnp.dot(t[0], cur[0, here, :], preferred_element_type=F32)
-                + jnp.dot(t[1], cur[1, here, :], preferred_element_type=F32))
+        return jnp.dot(t, cur[0, here, :], preferred_element_type=F32)
 
     def accumulate(k):
-        made = product(k, [t_v[k, half].reshape(chips * own_tok, width) for half in range(CORES)])
+        made = product(k, t_v[k, 0].reshape(chips * own_tok, width))
         acc[...] += made.reshape(acc.shape)
 
     def send_sums(bit, t):
@@ -216,8 +202,7 @@
     def reduce_step(i, t):
         part = pl.ds(t * block, block)
         if i == 0:
-            made = product(last, [
-                t_v[last, half, :, part, :].reshape(chips * block, width) for half in range(CORES)])
+            made = product(last, t_v[last, 0, :, part, :].reshape(chips * block, width))
             acc[:, part, :] += made.reshape(chips, block, kv)
         else:
             add_sums(bits[i - 1], t)
@@ -226,14 +211,9 @@
         else:
             p_send[0, t] = acc[z, part, :].astype(BF16)
 
-    def send_gradient(k):
-        gp_send[k] = partial_gradient(k, other).astype(BF16)
-        gp_copy(k).start()
-
     def finish_gradient(k):
         here = pl.ds(pl.multiple_of(k * width, width), width)
-        gp_copy(k).wait_recv()
-        gradient = (g_v[k] + gp_recv[k].astype(F32)) / rep_tok
+        gradient = partial_gradient(k, 0) / rep_tok
         velocity = MOMENT * m_v[here, :] + gradient
         m_v[here, :] = velocity
         stepped = b_v[here, :] - LEARN * (gradient + MOMENT * velocity)
@@ -252,7 +232,7 @@
         @pl.loop(0, last)
         def _(k):
             arrived(k)
-            send_gradient(k)
+            finish_gradient(k)
 
             @pl.when(k + look < last)
             def _():
@@ -262,12 +242,7 @@
             def _():
                 send_last()
 
-            g_v[k] = partial_gradient(k, c)
             accumulate(k)
-
-            @pl.when(k >= 1)
-            def _():
-                finish_gradient(k - 1)
 
             @pl.when(k >= 4)
             def _():
@@ -281,14 +256,10 @@
                 end_copy(t, half, j).wait_recv()
         reduce_step(0, t)
         if t == nt - 1:
-            send_gradient(last)
-            if last >= 1:
-                finish_gradient(last - 1)
-            g_v[last] = partial_gradient(last, c)
+            finish_gradient(last)
         for i in range(1, len(bits) + 1):
             if t >= i:
                 reduce_step(i, t - i)
-    finish_gradient(last)
     for k in range(max(0, last - 4), last):
         mix(k)
     for late in range(nt, nt + len(bits)):
@@ -313,9 +284,7 @@
                 tok_copy(k, half, j).wait_send()
             for t in range(nt):
                 end_copy(t, half, j).wait_send()
-    cur_copy.wait_send()
     for k in range(nk):
-        gp_copy(k).wait_send()
         s_copy(k).wait_send()
         for i in range(2):
             store(k, i).wait()
@@ -335,7 +304,7 @@
     any_spec = pl.BlockSpec(memory_space=pl.ANY)
     dma = pltpu.SemaphoreType.DMA
     return pl.pallas_call(
-        partial(push_kernel, 1 << level, chips, nk, 2),
+        partial(push_kernel, 1 << level, chips, nk, 3),
         out_shape=(
             jax.ShapeDtypeStruct((own_tok, kv), BF16),
             jax.ShapeDtypeStruct((rows, kv), F32),
@@ -356,14 +325,11 @@
             pltpu.VMEM((chips, nt, block, kv), BF16),
             pltpu.VMEM((nk, width, kv), BF16),
             pltpu.VMEM((nk, width, kv), BF16),
-            pltpu.VMEM((nk, width, kv), F32),
-            pltpu.VMEM((nk, width, kv), BF16),
-            pltpu.VMEM((nk, width, kv), BF16),
             pltpu.VMEM((8, 128), F32),
             pltpu.VMEM((8, 128), F32),
             dma((4,)), dma((nk, CORES)), dma((chips,)), dma((chips,)), dma((nk, CORES, n)), dma((nk, CORES, n)),
             dma((nt, CORES, n)), dma((nt, CORES, n)),
-            dma(()), dma(()), dma((nk,)), dma((nk,)), dma((nk,)), dma((nk,)), dma((chips, nt)), dma((chips, nt)),
+            dma((nk,)), dma((nk,)), dma((chips, nt)), dma((chips, nt)),
             dma(()), dma(()), dma((nk, 2)),
         ],
         compiler_params=pltpu.CompilerParams(

time: 85.9 us -> 83.6 us (0.973); the launches traced: 85.2 us -> 83.9 us
  Pallas kernels: 83.9 us -> 82.6 us
    pallas_call x1, Pallas kernels: 79.6 us -> 78.3 us  [push_call(): pl.pallas_call(partial(push_kernel, 1 << level, chips, nk, 3), out_shape=...]
where the time goes in v6:
time: 83.6 us; the launch traced here: 83.9 us
  Pallas kernels  82.6 us (99%)
  between operations  1.3 us (2%)
    pallas_call x1, Pallas kernels, push_call(): pl.pallas_call(partial(push_kernel, 1 << level, chips, nk, 3), out_shape=...  78.3 us
    pallas_call x1, Pallas kernels, hand_out(): pl.pallas_call(partial(hand_out_kernel, parts), out_shape=(like(p), like(...  4.36 us

profile of v6, /device:TPU:0, one launch (start us, length us, event | category | flops | bytes accessed | tf_op | source)
XLA Modules:
  0.0 83.9 jit_solution(9726517463423649641)
XLA Ops:
  1.3 78.3 %conditional.1 = ((bf16[128,512]{1,0:T(8,128)(2,1)S(1)}, f32[1024,512]{1,0:T(8,128)S(1)}, f32[8,128]{1,0:T(8,128)S(1)}, f32[1024,512]{1,0:T(8,128)})) conditional(s32[]{:T(128)} %clamp.3, (bf16[128,8192]{1,0:T(8,128)(2,1)}, bf16[128,512]{1,0:T(8,128)(2,1)}, f32[1024,512]{1,0:T(8,128)}, f32[1024,512]{1,0:T(8,128)}, f32[1]{0:T(128)}) %tuple.22, ...), branch_computations={%region_0.1_spmd, %region_1.2_spmd} | conditional | flops 2147483648 | bytes 6291464 | solution.py:409
  1.3 78.3 %push_round_1.1 = (bf16[128,512]{1,0:T(8,128)(2,1)S(1)}, f32[1024,512]{1,0:T(8,128)S(1)}, f32[8,128]{1,0:T(8,128)S(1)}, f32[1024,512]{1,0:T(8,128)}) custom-call(bf16[128,8192]{1,0:T(8,128)(2,1)} %get-tuple-element.25.tok, bf16[128,512]{1,0:T(8,128)(2,1)} %get-tuple-element.26.cot, f32[1024,512]{1,0:T(8,128)} %get-tuple-element.27.biased, ...), custom_call_target="tpu_custom_call" | custom-call | flops 2147483648 | bytes 6291456 | tf_op jit(solution)/shard_map/cond/branch_1_fun/push_round_1/pallas_call | solution.py:306
  79.6 4.4 %hand_out.1 = (bf16[128,512]{1,0:T(8,128)(2,1)}, f32[1024,512]{1,0:T(8,128)}, f32[1]{0:T(128)}, f32[1024,512]{1,0:T(8,128)}, f32[1024,512]{1,0:T(8,128)}) custom-call(bf16[128,512]{1,0:T(8,128)(2,1)S(1)} %get-tuple-element.44.p, f32[1024,512]{1,0:T(8,128)S(1)} %get-tuple-element.45.mix, f32[8,128]{1,0:T(8,128)S(1)} %get-tuple-element.46.w, ...), custom_call_target="tpu_custom_call" | custom-call | bytes 6291456 | tf_op jit(solution)/shard_map/hand_out/pallas_call | solution.py:391
